TPU v7x, 32 devices: a whole 2x2x4 slice. The times are simulated.
32 devices in a mesh: group: 4 (over y, x), dp: 2 (over core), mp: 4 (over z).
Axes of the slice: x: 2, y: 2, z: 4, core: 2. Of those that a mesh axis runs over, the one named last changes fastest.
Arguments:
- block_input: bfloat16 [96, 8192], P(None, 'dp'), may hold values from -6 to 6
- parent_gate_up: bfloat16 [2, 8192, 14336], P(None, 'dp', ('group', 'mp')), may hold values from -0.0625 to 0.0625
- parent_down: bfloat16 [14336, 8192], P(('group', 'mp'), 'dp'), may hold values from -0.046875 to 0.046875
- variant_gate_up: bfloat16 [4, 2, 8192, 3584], P('group', None, 'dp', 'mp'), may hold values from -0.0625 to 0.0625
- variant_down: bfloat16 [4, 3584, 8192], P('group', 'mp', 'dp'), may hold values from -0.09375 to 0.09375
- widths: int32 [4], P('group'), may hold values from 896 to 3584, as said below
Outputs:
- grad_gate_up: float32 [4, 2, 8192, 3584], P('group', None, 'dp', 'mp')
- grad_down: float32 [4, 3584, 8192], P('group', 'mp', 'dp')
Inputs may be any that keep to these rules, and one draw needn't show every extreme that they name: Variant v uses its hidden units 0 to widths[v] - 1; one variant uses all 3584 of them and another exactly a quarter of 3584.
All inputs are finite; a program needn't handle non-finite values.
Results may differ from a plain program's by a relative error of at most 0.008.
Values may be sent and summed in bfloat16 or wider, within the bound.
A program may use at most 192 MiB of HBM per device.

v0:
```python
import math

import jax
import jax.numpy as jnp
from jax import lax
from jax.sharding import PartitionSpec as P


def gated_values(pre_act, unit_mask):
    gate_value = pre_act[:, 0].astype(jnp.float32)
    up_value = pre_act[:, 1].astype(jnp.float32)
    sigmoid_gate = jax.nn.sigmoid(gate_value)
    return (gate_value * sigmoid_gate * up_value * unit_mask).astype(jnp.bfloat16)


def pre_gradient(pre_act, unit_mask, hidden_grad):
    gate_value = pre_act[:, 0].astype(jnp.float32)
    up_value = pre_act[:, 1].astype(jnp.float32)
    sigmoid_gate = jax.nn.sigmoid(gate_value)
    masked_grad = hidden_grad * unit_mask
    grad_gate = masked_grad * up_value * sigmoid_gate * (1.0 + gate_value * (1.0 - sigmoid_gate))
    grad_up = masked_grad * gate_value * sigmoid_gate
    return jnp.stack([grad_gate, grad_up], axis=1).astype(jnp.bfloat16)


def body(block_input, parent_gate_up, parent_down, variant_gate_up, variant_down, widths):
    local_gate_up = variant_gate_up[0]
    local_down = variant_down[0]
    local_units = local_down.shape[0]
    all_tokens = block_input.shape[0]
    first_unit = lax.axis_index("mp") * local_units
    unit_index = first_unit + jnp.arange(local_units, dtype=jnp.int32)
    unit_mask = (unit_index < widths[0]).astype(jnp.float32)
    parent_term = jnp.einsum(
        "td,kdf->tkf", block_input, parent_gate_up, preferred_element_type=jnp.float32
    )
    variant_term = jnp.einsum(
        "td,kdf->tkf", block_input, local_gate_up, preferred_element_type=jnp.float32
    )
    parent_rows, variant_rows = (
        lax.psum_scatter(parent_term, "dp", scatter_dimension=0, tiled=True),
        lax.psum_scatter(variant_term, "dp", scatter_dimension=0, tiled=True),
    )
    parent_pre = parent_rows.astype(jnp.bfloat16)
    variant_pre = variant_rows.astype(jnp.bfloat16)
    parent_hidden = gated_values(parent_pre, 1.0)
    variant_own = gated_values(variant_pre, unit_mask)
    parent_all, variant_hidden = (
        lax.all_gather(parent_hidden, "dp", axis=0, tiled=True),
        lax.all_gather(variant_own, "dp", axis=0, tiled=True),
    )
    teacher_part = jnp.dot(parent_all, parent_down, preferred_element_type=jnp.float32)
    student_part = jnp.dot(variant_hidden, local_down, preferred_element_type=jnp.float32)
    teacher = lax.psum(teacher_part, ("group", "mp"))
    student = lax.psum(student_part, "mp")
    loss_scale = 1.0 / math.sqrt(all_tokens)
    output_grad = ((student - teacher) * loss_scale).astype(jnp.bfloat16)
    grad_down = lax.dot_general(
        variant_hidden, output_grad, (((0,), (0,)), ((), ())), preferred_element_type=jnp.float32
    )
    hidden_part = lax.dot_general(
        output_grad, local_down, (((1,), (1,)), ((), ())), preferred_element_type=jnp.float32
    )
    hidden_own = lax.psum_scatter(hidden_part, "dp", scatter_dimension=0, tiled=True)
    grad_own = pre_gradient(variant_pre, unit_mask, hidden_own)
    grad_pre = lax.all_gather(grad_own, "dp", axis=0, tiled=True)
    grad_gate_up = jnp.einsum(
        "td,tkf->kdf", block_input, grad_pre, preferred_element_type=jnp.float32
    )
    return (grad_gate_up[None], grad_down[None])


def solution(mesh):
    in_specs = (
        P(None, "dp"),
        P(None, "dp", ("group", "mp")),
        P(("group", "mp"), "dp"),
        P("group", None, "dp", "mp"),
        P("group", "mp", "dp"),
        P("group"),
    )
    out_specs = (P("group", None, "dp", "mp"), P("group", "mp", "dp"))
    return jax.shard_map(body, mesh=mesh, in_specs=in_specs, out_specs=out_specs, check_vma=False)
```

profile of v0, /device:TPU:0, one launch (start us, length us, event | category | flops | bytes accessed | tf_op | source)
XLA Modules:
  0.0 303.7 jit_solution(10510049794783898362)
XLA Ops:
  7.2 0.0 copy-start
  7.2 0.0 reduce-scatter.4.cloned.1.call-start
  7.2 1.1 copy-done
  8.3 8.5 %fusion = f32[96,2,896]{2,0,1:T(8,128)} fusion(bf16[1,2,4096,896]{3,2,1,0:T(8,128)(2,1)} %param.9, bf16[96,4096]{1,0:T(8,128)(2,1)S(1)} %copy-done), kind=kOutput, calls=%fused_computation | convolution fusion | flops 1409286144 | bytes 16154624 | tf_op jit(solution)/shard_map/td,kdf->tkf/dot_general | solution.py:37
  16.8 0.0 reduce-scatter.4.cloned.1.call-update
  16.8 0.0 reduce-scatter.6.cloned.1.call-start
  16.8 8.5 %fusion.7 = f32[96,2,896]{2,0,1:T(8,128)} fusion(bf16[2,4096,896]{2,1,0:T(8,128)(2,1)} %param.7, bf16[96,4096]{1,0:T(8,128)(2,1)S(1)} %copy-done), kind=kOutput, calls=%fused_computation.10 | convolution fusion | flops 1409286144 | bytes 16154624 | tf_op jit(solution)/shard_map/td,kdf->tkf/dot_general | solution.py:34
  25.3 0.0 reduce-scatter.6.cloned.1.call-update
  25.3 0.0 all-reduce.3.cloned.1.call-start
  26.0 1.9 reduce-scatter.4.cloned.1.call-done
  27.9 1.0 convert_element_type.49
  28.9 0.1 fusion.15
  29.0 1.9 all_gather.9
  30.9 5.6 %fusion.4 = f32[96,4096]{1,0:T(8,128)} fusion(bf16[96,896]{1,0:T(8,128)(2,1)S(1)} %all_gather.9, bf16[1,896,4096]{2,1,0:T(8,128)(2,1)} %param.10), kind=kOutput, calls=%fused_computation.6 | convolution fusion | flops 704643072 | bytes 9084928 | tf_op jit(solution)/shard_map/dot_general | solution.py:53
  36.5 0.0 all-reduce.3.cloned.1.call-update
  36.5 0.0 all-reduce.5.cloned.1.call-start
  36.6 3.4 %reduce-scatter.6.cloned.1.call-done = f32[48,2,896]{2,0,1:T(8,128)} async-done(((f32[96,2,896]{2,0,1:T(8,128)}), f32[48,2,896]{2,0,1:T(8,128)}) %reduce-scatter.6.cloned.1.call-update) | async-done | bytes 344080 | tf_op jit(solution)/shard_map/reduce_scatter | solution.py:41
  40.0 1.0 convert_element_type.56
  41.0 0.1 fusion.25
  41.1 1.9 all_gather.10
  43.0 5.6 %fusion.29 = f32[96,4096]{1,0:T(8,128)} fusion(bf16[96,896]{1,0:T(8,128)(2,1)S(1)} %all_gather.10, bf16[896,4096]{1,0:T(8,128)(2,1)} %param.8), kind=kOutput, calls=%fused_computation.46 | convolution fusion | flops 704643072 | bytes 9084928 | tf_op jit(solution)/shard_map/dot_general | solution.py:52
  48.7 0.0 all-reduce.5.cloned.1.call-update
  48.7 0.0 reduce-scatter.8.cloned.1.call-start
  48.7 64.6 %all-reduce.3.cloned.1.call-done = f32[96,4096]{1,0:T(8,128)} async-done(((f32[96,4096]{1,0:T(8,128)}), f32[96,4096]{1,0:T(8,128)}) %all-reduce.3.cloned.1.call-update) | async-done | bytes 1572880 | tf_op jit(solution)/shard_map/psum | solution.py:55
  113.3 122.2 %all-reduce.5.cloned.1.call-done = f32[96,4096]{1,0:T(8,128)} async-done(((f32[96,4096]{1,0:T(8,128)}), f32[96,4096]{1,0:T(8,128)}) %all-reduce.5.cloned.1.call-update) | async-done | bytes 1572880 | tf_op jit(solution)/shard_map/psum | solution.py:54
  235.5 2.1 multiply_convert_fusion
  237.6 6.1 %fusion.2 = f32[96,896]{1,0:T(8,128)} fusion(bf16[96,4096]{1,0:T(8,128)(2,1)S(1)} %multiply_convert_fusion, bf16[1,896,4096]{2,1,0:T(8,128)(2,1)} %param.10), kind=kOutput, calls=%fused_computation.4 | convolution fusion | flops 704643072 | bytes 8470528 | tf_op jit(solution)/shard_map/dot_general | solution.py:61
  243.8 0.0 reduce-scatter.8.cloned.1.call-update
  243.8 7.6 %convolution_bitcast_fusion.1 = f32[1,896,4096]{2,1,0:T(8,128)} fusion(bf16[96,896]{1,0:T(8,128)(2,1)S(1)} %all_gather.9, bf16[96,4096]{1,0:T(8,128)(2,1)S(1)} %multiply_convert_fusion), kind=kOutput, calls=%fused_computation.3 | convolution fusion | flops 704643072 | bytes 15638528 | tf_op jit(solution)/shard_map/dot_general | solution.py:58
  251.4 0.0 reduce-scatter.8.cloned.1.call-done
  251.4 1.0 fusion.27
  252.4 2.1 all_gather.11
  254.5 11.7 %convolution_bitcast_fusion = f32[1,2,4096,896]{2,3,1,0:T(8,128)} fusion(bf16[96,2,896]{2,0,1:T(8,128)(2,1)S(1)} %all_gather.11, bf16[96,4096]{1,0:T(8,128)(2,1)S(1)} %copy-done), kind=kOutput, calls=%fused_computation.2 | convolution fusion | flops 1409286144 | bytes 30490624 | tf_op jit(solution)/shard_map/td,tkf->kdf/dot_general | solution.py:67
  266.1 0.0 copy-start.1
  266.1 31.0 %copy.8 = f32[1,2,4096,896]{3,2,1,0:T(8,128)} copy(f32[1,2,4096,896]{2,3,1,0:T(8,128)} %convolution_bitcast_fusion) | data formatting | bytes 58720256
  297.1 0.0 copy-done.1
  (2 shorter events, 0.0 us)
Async XLA Ops:
  7.2 1.1 copy-start
  7.2 20.7 %reduce-scatter.4.cloned.1.call-start = ((), (), s32[]{:S(2)}) async-start(), calls=%async_computation.3 | async-start | bytes 1032192 | tf_op jit(solution)/shard_map/reduce_scatter | solution.py:42
  16.8 23.2 %reduce-scatter.6.cloned.1.call-start = ((), (), s32[]{:S(2)}) async-start(), calls=%async_computation.5 | async-start | bytes 1032192 | tf_op jit(solution)/shard_map/reduce_scatter | solution.py:41
  25.3 88.0 %all-reduce.3.cloned.1.call-start = ((), (), s32[]{:S(2)}) async-start(), calls=%async_computation.4 | async-start | bytes 3145728 | tf_op jit(solution)/shard_map/psum | solution.py:55
  36.5 199.0 %all-reduce.5.cloned.1.call-start = ((), (), s32[]{:S(2)}) async-start(), calls=%async_computation.6 | async-start | bytes 3145728 | tf_op jit(solution)/shard_map/psum | solution.py:54
  48.7 202.7 %reduce-scatter.8.cloned.1.call-start = ((), (), s32[]{:S(2)}) async-start(), calls=%async_computation.7 | async-start | bytes 516096 | tf_op jit(solution)/shard_map/reduce_scatter | solution.py:64
  266.1 31.0 %copy-start.1 = (bf16[96,4096]{1,0:T(8,128)(2,1)S(1)}, bf16[96,4096]{1,0:T(8,128)(2,1)}, u32[]{:S(2)}) copy-start(bf16[96,4096]{1,0:T(8,128)(2,1)} %param.6) | copy-start | bytes 2359300
Sparse Core Ops, SparseCore 0:
  16.9 10.9 reduce-scatter.3
  30.7 9.2 reduce-scatter.5
  43.0 70.2 all-reduce.2
  119.1 116.3 all-reduce.4
  243.9 7.0 reduce-scatter.7
where the time goes:
time: 305 us; the launch traced here: 304 us
  waiting for transfers between devices  192 us (63%)
  matrix products  53.6 us (18%)
  local copies, waits for them, and re-layouts  32.1 us (11%)
  between operations  14.5 us (5%)
  blocking collectives  5.91 us (2%)
  other arithmetic  5.23 us (2%)
    psum x1, waiting for transfers between devices, body(): teacher = lax.psum(teacher_part, ('group', 'mp'))  122 us
    psum x1, waiting for transfers between devices, body(): student = lax.psum(student_part, 'mp')  64.6 us
    unnamed x5, local copies, waits for them, and re-layouts  32.1 us
    dot_general x1, matrix products, body(): jnp.einsum('td,tkf->kdf', block_input, grad_pre, preferred_element_type=j...  11.7 us
    dot_general x1, matrix products, body(): jnp.einsum('td,kdf->tkf', block_input, parent_gate_up, preferred_element_...  8.47 us
    dot_general x1, matrix products, body(): jnp.einsum('td,kdf->tkf', block_input, local_gate_up, preferred_element_t...  8.46 us
    dot_general x1, matrix products, body(): lax.dot_general(variant_hidden, output_grad, (((0,), (0,)), ((), ())), pr...  7.57 us
    dot_general x1, matrix products, body(): lax.dot_general(output_grad, local_down, (((1,), (1,)), ((), ())), prefer...  6.15 us
  transfers between devices with their start and end apart: 5, of which 4 were waited for; matrix products, arithmetic and copies ran while one was open for 10% of the time, Pallas kernels for 0%

commit v1 on v0

--- a/solution.py
+++ b/solution.py
@@ -1,8 +1,11 @@
+import functools
 import math
 
 import jax
 import jax.numpy as jnp
 from jax import lax
+from jax.experimental import pallas as pl
+from jax.experimental.pallas import tpu as pltpu
 from jax.sharding import PartitionSpec as P
 
 
@@ -23,7 +26,7 @@
     return jnp.stack([grad_gate, grad_up], axis=1).astype(jnp.bfloat16)
 
 
-def body(block_input, parent_gate_up, parent_down, variant_gate_up, variant_down, widths):
+def plain_body(block_input, parent_gate_up, parent_down, variant_gate_up, variant_down, widths):
     local_gate_up = variant_gate_up[0]
     local_down = variant_down[0]
     local_units = local_down.shape[0]
@@ -70,6 +73,349 @@
     return (grad_gate_up[None], grad_down[None])
 
 
+VMEM_BYTES = 60 * 1024 * 1024
+AXES = ("group", "dp", "mp")
+NT = (((1,), (1,)), ((), ()))
+TN = (((0,), (0,)), ((), ()))
+
+
+def fused_kernel(
+    sizes,
+    x_ref, mask_ref, wp_hbm, pd_hbm, wv_hbm, vd_hbm,
+    vh_ref, o_ref, gp_ref,
+    wp, pd, wv, vd,
+    acc_v, acc_p, got_v, got_p, pre_v, ph,
+    s_part, s_own, s_got, t_part, t_own, t_got, q_part, q_own, q_got, t_all, o_all, h_acc, h_got,
+    wp_sem, pd_sem, wv_sem, vd_sem,
+    av_s, av_r, ap_s, ap_r, s_s, s_r, t_s, t_r, q_s, q_r, b_s, b_r, o_s, o_r, h_s, h_r,
+):
+    f32, bf16 = jnp.float32, jnp.bfloat16
+    index = {axis: lax.axis_index(axis) for axis in AXES}
+    tokens, width = x_ref.shape
+    n_group, n_dp, n_mp = (sizes[axis] for axis in AXES)
+    piece = o_all.shape[-1]
+    k_rows = width // (wv_sem.shape[0] // 2)
+    k_steps = width // k_rows
+    block = math.gcd(tokens, 32)
+    g, m = index["group"], index["mp"]
+    sent = []
+
+    def peer(axis, step):
+        return lax.rem(index[axis] + step, sizes[axis])
+
+    def send(src, dst, send_sem, recv_sem, axis, step):
+        copy = pltpu.make_async_remote_copy(
+            src_ref=src, dst_ref=dst, send_sem=send_sem, recv_sem=recv_sem,
+            device_id={axis: peer(axis, step)}, device_id_type=pl.DeviceIdType.MESH,
+        )
+        copy.start()
+        sent.append(copy)
+        return copy
+
+    def columns(q, z):
+        return pl.ds(pl.multiple_of((q * n_mp + z) * piece, piece), piece)
+
+    def rows_loop(step_fn):
+        @pl.loop(0, tokens // block)
+        def _(i):
+            step_fn(pl.ds(pl.multiple_of(i * block, block), block))
+
+    def gate_up_copy(hbm, buf, sem, i):
+        rows = pl.ds(pl.multiple_of(lax.rem(i, k_steps) * k_rows, k_rows), k_rows)
+        k = i // k_steps
+        return pltpu.make_async_copy(hbm.at[k, rows], buf.at[k, rows], sem.at[i])
+
+    def down_copy(hbm, buf, sem, i):
+        n_rows = buf.shape[0] // sem.shape[0]
+        rows = pl.ds(i * n_rows, n_rows)
+        return pltpu.make_async_copy(hbm.at[rows], buf.at[rows], sem.at[i])
+
+    for i in range(2 * k_steps):
+        gate_up_copy(wv_hbm, wv, wv_sem, i).start()
+    for i in range(vd_sem.shape[0]):
+        down_copy(vd_hbm, vd, vd_sem, i).start()
+
+    barrier = pltpu.get_barrier_semaphore()
+    for axis in AXES:
+        for step in range(1, sizes[axis]):
+            pl.semaphore_signal(
+                barrier, inc=1, device_id={axis: peer(axis, step)},
+                device_id_type=pl.DeviceIdType.MESH,
+            )
+    pl.semaphore_wait(barrier, n_group + n_dp + n_mp - 3)
+
+    def pre_activations(hbm, buf, sem, acc, got, send_sem, recv_sem, after):
+        copies = []
+        for k in range(2):
+            @pl.loop(0, k_steps)
+            def _(r):
+                i = k * k_steps + r
+                gate_up_copy(hbm, buf, sem, i).wait()
+                after(i)
+                rows = pl.ds(pl.multiple_of(r * k_rows, k_rows), k_rows)
+                term = jnp.dot(x_ref[:, rows], buf[k, rows, :], preferred_element_type=f32)
+
+                @pl.when(r == 0)
+                def _():
+                    acc[k] = term
+
+                @pl.when(r > 0)
+                def _():
+                    acc[k] += term
+            for step in range(1, n_dp):
+                slot = (step - 1) * 2 + k
+                copies.append(send(
+                    acc.at[k], got.at[slot], send_sem.at[slot], recv_sem.at[slot], "dp", step))
+        return copies
+
+    def total_pre(acc, got, k, rows):
+        value = acc[k, rows, :]
+        for step in range(n_dp - 1):
+            value = value + got[step * 2 + k, rows, :]
+        return value.astype(bf16)
+
+    def start_parent(i):
+        gate_up_copy(wp_hbm, wp, wp_sem, i).start()
+
+    for copy in pre_activations(wv_hbm, wv, wv_sem, acc_v, got_v, av_s, av_r, start_parent):
+        copy.wait_recv()
+    for i in range(pd_sem.shape[0]):
+        down_copy(pd_hbm, pd, pd_sem, i).start()
+
+    def variant_rows(rows):
+        gate, up = total_pre(acc_v, got_v, 0, rows), total_pre(acc_v, got_v, 1, rows)
+        pre_v[0, rows, :] = gate
+        pre_v[1, rows, :] = up
+        gate, up = gate.astype(f32), up.astype(f32)
+        vh_ref[rows, :] = (gate * jax.nn.sigmoid(gate) * up * mask_ref[...]).astype(bf16)
+
+    rows_loop(variant_rows)
+    for i in range(vd_sem.shape[0]):
+        down_copy(vd_hbm, vd, vd_sem, i).wait()
+
+    s_copies = []
+    for step in list(range(1, n_mp)) + [0]:
+        z = peer("mp", step)
+
+        @pl.loop(0, n_group)
+        def _(q):
+            term = jnp.dot(vh_ref[...], vd[:, columns(q, z)], preferred_element_type=f32)
+            if step == 0:
+                s_own[q] = term
+            else:
+                s_part[step - 1, q] = term.astype(bf16)
+        if step:
+            s_copies.append(send(
+                s_part.at[step - 1], s_got.at[step - 1], s_s.at[step - 1], s_r.at[step - 1],
+                "mp", step))
+
+    for copy in pre_activations(wp_hbm, wp, wp_sem, acc_p, got_p, ap_s, ap_r, lambda i: None):
+        copy.wait_recv()
+
+    def parent_rows(rows):
+        gate = total_pre(acc_p, got_p, 0, rows).astype(f32)
+        up = total_pre(acc_p, got_p, 1, rows).astype(f32)
+        ph[rows, :] = (gate * jax.nn.sigmoid(gate) * up).astype(bf16)
+
+    rows_loop(parent_rows)
+    for i in range(pd_sem.shape[0]):
+        down_copy(pd_hbm, pd, pd_sem, i).wait()
+
+    t_copies = []
+    for step in list(range(1, n_group)) + [0]:
+        q = peer("group", step)
+
+        @pl.loop(0, n_mp)
+        def _(z):
+            term = jnp.dot(ph[...], pd[:, columns(q, z)], preferred_element_type=f32)
+            if step == 0:
+                t_own[z] = term
+            else:
+                t_part[step - 1, z] = term.astype(bf16)
+        if step:
+            t_copies.append(send(
+                t_part.at[step - 1], t_got.at[step - 1], t_s.at[step - 1], t_r.at[step - 1],
+                "group", step))
+
+    for copy in t_copies:
+        copy.wait_recv()
+    q_copies = []
+    for step in list(range(1, n_mp)) + [0]:
+        z = peer("mp", step)
+        value = t_own[z]
+        for other in range(n_group - 1):
+            value = value + t_got[other, z].astype(f32)
+        if step == 0:
+            q_own[...] = value
+        else:
+            q_part[step - 1] = value.astype(bf16)
+            q_copies.append(send(
+                q_part.at[step - 1], q_got.at[step - 1], q_s.at[step - 1], q_r.at[step - 1],
+                "mp", step))
+    for copy in q_copies:
+        copy.wait_recv()
+    value = q_own[...]
+    for other in range(n_mp - 1):
+        value = value + q_got[other].astype(f32)
+    t_all[g] = value.astype(bf16)
+    b_copies = [
+        send(t_all.at[g], t_all.at[g], b_s.at[step - 1], b_r.at[step - 1], "group", step)
+        for step in range(1, n_group)
+    ]
+    for copy in s_copies + b_copies:
+        copy.wait_recv()
+
+    loss_scale = 1.0 / math.sqrt(tokens)
+
+    @pl.loop(0, n_group)
+    def _(q):
+        student = s_own[q]
+        for other in range(n_mp - 1):
+            student = student + s_got[other, q].astype(f32)
+        o_all[m, q] = ((student - t_all[q].astype(f32)) * loss_scale).astype(bf16)
+
+    o_copies = [
+        send(o_all.at[m], o_all.at[m], o_s.at[step - 1], o_r.at[step - 1], "mp", step)
+        for step in range(1, n_mp)
+    ]
+    for step in range(n_mp):
+        z = peer("mp", n_mp - step)
+        if step:
+            o_copies[step - 1].wait_recv()
+
+        @pl.loop(0, n_group)
+        def _(q):
+            part = o_all[z, q]
+            o_ref[:, columns(q, z)] = part
+            term = lax.dot_general(part, vd[:, columns(q, z)], NT, preferred_element_type=f32)
+            if step == 0:
+                @pl.when(q == 0)
+                def _():
+                    h_acc[...] = term
+
+                @pl.when(q > 0)
+                def _():
+                    h_acc[...] += term
+            else:
+                h_acc[...] += term
+
+    h_copies = [
+        send(h_acc, h_got.at[step - 1], h_s.at[step - 1], h_r.at[step - 1], "dp", step)
+        for step in range(1, n_dp)
+    ]
+    for copy in h_copies:
+        copy.wait_recv()
+
+    def gradient_rows(rows):
+        hidden = h_acc[rows, :]
+        for other in range(n_dp - 1):
+            hidden = hidden + h_got[other, rows, :]
+        gate, up = pre_v[0, rows, :].astype(f32), pre_v[1, rows, :].astype(f32)
+        sig = jax.nn.sigmoid(gate)
+        masked = hidden * mask_ref[...]
+        gp_ref[0, rows, :] = (masked * up * sig * (1.0 + gate * (1.0 - sig))).astype(bf16)
+        gp_ref[1, rows, :] = (masked * gate * sig).astype(bf16)
+
+    rows_loop(gradient_rows)
+    for copy in sent:
+        copy.wait_send()
+
+
+def layout(sizes, tokens, width, p_units, v_units):
+    f32, bf16 = jnp.float32, jnp.bfloat16
+    n_group, n_dp, n_mp = (sizes[axis] for axis in AXES)
+    piece = width // (n_group * n_mp)
+    k_steps = width // math.gcd(width, 1024)
+    v, dma = pltpu.VMEM, pltpu.SemaphoreType.DMA
+    buffers = [
+        v((2, width, p_units), bf16), v((p_units, width), bf16),
+        v((2, width, v_units), bf16), v((v_units, width), bf16),
+        v((2, tokens, v_units), f32), v((2, tokens, p_units), f32),
+        v((2 * (n_dp - 1), tokens, v_units), f32), v((2 * (n_dp - 1), tokens, p_units), f32),
+        v((2, tokens, v_units), bf16), v((tokens, p_units), bf16),
+        v((n_mp - 1, n_group, tokens, piece), bf16), v((n_group, tokens, piece), f32),
+        v((n_mp - 1, n_group, tokens, piece), bf16),
+        v((n_group - 1, n_mp, tokens, piece), bf16), v((n_mp, tokens, piece), f32),
+        v((n_group - 1, n_mp, tokens, piece), bf16),
+        v((n_mp - 1, tokens, piece), bf16), v((tokens, piece), f32),
+        v((n_mp - 1, tokens, piece), bf16),
+        v((n_group, tokens, piece), bf16), v((n_mp, n_group, tokens, piece), bf16),
+        v((tokens, v_units), f32), v((n_dp - 1, tokens, v_units), f32),
+    ]
+    down = 4
+    d2, d1, g1, m1 = 2 * (n_dp - 1), n_dp - 1, n_group - 1, n_mp - 1
+    counts = [2 * k_steps, down, 2 * k_steps, down]
+    for n in (d2, d2, m1, g1, m1, g1, m1, d1):
+        counts += [n, n]
+    return buffers, [dma((n,)) for n in counts]
+
+
+def fused_fits(sizes, tokens, width, p_units, v_units):
+    if min(sizes[axis] for axis in AXES) < 2:
+        return False
+    piece = width // (sizes["group"] * sizes["mp"])
+    if piece % 128 or tokens % 16 or p_units % 128 or v_units % 128:
+        return False
+    buffers, _ = layout(sizes, tokens, width, p_units, v_units)
+    held = sum(math.prod(b.shape) * jnp.dtype(b.dtype).itemsize for b in buffers)
+    held += 2 * tokens * (2 * width + 3 * v_units)
+    return held <= VMEM_BYTES - 3 * 1024 * 1024
+
+
+def matmul_tn_kernel(a_ref, b_ref, out_ref):
+    out_ref[...] = lax.dot_general(a_ref[...], b_ref[...], TN, preferred_element_type=jnp.float32)
+
+
+def outer_product(a, b, rows):
+    tokens, n_rows = a.shape
+    members, _, n_columns = b.shape
+    rows = math.gcd(n_rows, rows)
+    return pl.pallas_call(
+        matmul_tn_kernel,
+        grid=(members, n_rows // rows),
+        out_shape=jax.ShapeDtypeStruct((members, n_rows, n_columns), jnp.float32),
+        in_specs=[
+            pl.BlockSpec((tokens, rows), lambda k, i: (0, i)),
+            pl.BlockSpec((None, tokens, n_columns), lambda k, i: (k, 0, 0)),
+        ],
+        out_specs=pl.BlockSpec((None, rows, n_columns), lambda k, i: (k, i, 0)),
+        compiler_params=pltpu.CompilerParams(vmem_limit_bytes=32 * 1024 * 1024),
+    )(a, b)
+
+
+def fused_body(sizes, block_input, parent_gate_up, parent_down, variant_gate_up, variant_down, widths):
+    tokens, width = block_input.shape
+    p_units, v_units = parent_down.shape[0], variant_down.shape[1]
+    buffers, semaphores = layout(sizes, tokens, width, p_units, v_units)
+    unit_index = lax.axis_index("mp") * v_units + jnp.arange(v_units, dtype=jnp.int32)
+    unit_mask = (unit_index < widths[0]).astype(jnp.float32)[None]
+    vmem, anywhere = pl.BlockSpec(memory_space=pltpu.VMEM), pl.BlockSpec(memory_space=pl.ANY)
+    hidden, output_grad, pre_grad = pl.pallas_call(
+        functools.partial(fused_kernel, sizes),
+        out_shape=(
+            jax.ShapeDtypeStruct((tokens, v_units), jnp.bfloat16),
+            jax.ShapeDtypeStruct((tokens, width), jnp.bfloat16),
+            jax.ShapeDtypeStruct((2, tokens, v_units), jnp.bfloat16),
+        ),
+        in_specs=[vmem, vmem, anywhere, anywhere, anywhere, anywhere],
+        out_specs=(vmem, vmem, vmem),
+        scratch_shapes=buffers + semaphores,
+        compiler_params=pltpu.CompilerParams(
+            collective_id=0, has_side_effects=True, vmem_limit_bytes=VMEM_BYTES
+        ),
+    )(block_input, unit_mask, parent_gate_up, parent_down, variant_gate_up[0], variant_down[0])
+    grad_down = outer_product(hidden, output_grad[None], 128)
+    grad_gate_up = outer_product(block_input, pre_grad, 512)
+    return (grad_gate_up[None], grad_down)
+
+
+def body(sizes, *args):
+    tokens, width = args[0].shape
+    if fused_fits(sizes, tokens, width, args[2].shape[0], args[4].shape[1]):
+        return fused_body(sizes, *args)
+    return plain_body(*args)
+
+
 def solution(mesh):
     in_specs = (
         P(None, "dp"),
@@ -80,4 +426,7 @@
         P("group"),
     )
     out_specs = (P("group", None, "dp", "mp"), P("group", "mp", "dp"))
-    return jax.shard_map(body, mesh=mesh, in_specs=in_specs, out_specs=out_specs, check_vma=False)
+    return jax.shard_map(
+        functools.partial(body, dict(mesh.shape)),
+        mesh=mesh, in_specs=in_specs, out_specs=out_specs, check_vma=False,
+    )

time: 305 us -> 89.4 us (0.29)
  waiting for transfers between devices: 192 us -> 0 us
  Pallas kernels: 0 us -> 83.9 us
  matrix products: 53.6 us -> 0 us
  local copies, waits for them, and re-layouts: 32.1 us -> 2.13 us
  between operations: 14.5 us -> 1.31 us
  blocking collectives: 5.91 us -> 0 us
  other arithmetic: 5.23 us -> 0.59 us
    psum x2 -> x0, waiting for transfers between devices: 187 us -> none  [the longest x1 122 us: body(): teacher = lax.psum(teacher_part, ('group', 'mp'))]
    pallas_call x0 -> x3, Pallas kernels: none -> 83.9 us  [the longest x1 62.9 us: fused_body(): pl.pallas_call(functools.partial(fused_kernel, sizes), out_shape=(jax.Sha...]
    dot_general x7 -> x0, matrix products: 53.6 us -> none  [the longest x1 11.7 us: body(): jnp.einsum('td,tkf->kdf', block_input, grad_pre, preferred_element_type=j...]
    unnamed x5 -> x8, local copies, waits for them, and re-layouts: 32.1 us -> 2.13 us
    all_gather x3 -> x0, blocking collectives: 5.91 us -> none  [the longest x1 2.05 us: body(): grad_pre = lax.all_gather(grad_own, 'dp', axis=0, tiled=True)]
    reduce_scatter x3 -> x0, waiting for transfers between devices: 5.3 us -> none  [the longest x1 3.43 us: body(): lax.psum_scatter(parent_term, 'dp', scatter_dimension=0, tiled=True)]
    convert_element_type x6 -> x1, other arithmetic: 4.19 us -> 0.59 us  [fused_body(): unit_mask = (unit_index < widths[0]).astype(jnp.float32)[None]]
  transfers between devices with their start and end apart: 5 -> 0, of which waited for: 4 -> 0; matrix products, arithmetic and copies ran while one was open for 10% -> 0% of each run, Pallas kernels for 0% -> 0%
where the time goes in v1:
time: 89.4 us; the launch traced here: 87.9 us
  Pallas kernels  83.9 us (94%)
  local copies, waits for them, and re-layouts  2.13 us (2%)
  between operations  1.31 us (1%)
    pallas_call x1, Pallas kernels, fused_body(): pl.pallas_call(functools.partial(fused_kernel, sizes), out_shape=(jax.Sha...  62.9 us
    pallas_call x2, Pallas kernels, outer_product(): pl.pallas_call(matmul_tn_kernel, grid=(members, n_rows // rows), out_shap...  21 us
    unnamed x8, local copies, waits for them, and re-layouts  2.13 us

profile of v1, /device:TPU:0, one launch (start us, length us, event | category | flops | bytes accessed | tf_op | source)
XLA Modules:
  0.0 87.9 jit_solution(15658849108446059188)
XLA Ops:
  1.3 0.6 compare_convert_fusion.mask_ref
  1.9 62.9 %shard_map.77 = (bf16[96,896]{1,0:T(8,128)(2,1)}, bf16[96,4096]{1,0:T(8,128)(2,1)}, bf16[2,96,896]{2,1,0:T(8,128)(2,1)}) custom-call(bf16[96,4096]{1,0:T(8,128)(2,1)} %a_ref.1, f32[1,896]{1,0:T(1,128)} %compare_convert_fusion.mask_ref, bf16[2,4096,896]{2,1,0:T(8,128)(2,1)} %wp_hbm.1, bf16[896,4096]{1,0:T(8,128)(2,1)} %pd_hbm.1, ...), custom_call_target="tpu_custom_call" | custom-call | tf_op jit(solution)/shard_map/pallas_call | solution.py:393
  64.7 0.0 copy-start
  64.8 0.0 copy-start.1
  64.8 1.2 %copy-done.1 = bf16[96,4096]{1,0:T(8,128)(2,1)S(1)} copy-done((bf16[96,4096]{1,0:T(8,128)(2,1)S(1)}, bf16[96,4096]{1,0:T(8,128)(2,1)}, u32[]{:S(2)}) %copy-start.1) | copy-done | bytes 786456
  66.0 0.0 copy-start.3
  66.0 0.9 %copy-done.3 = bf16[96,896]{1,0:T(8,128)(2,1)S(1)} copy-done((bf16[96,896]{1,0:T(8,128)(2,1)S(1)}, bf16[96,896]{1,0:T(8,128)(2,1)}, u32[]{:S(2)}) %copy-start.3) | copy-done | bytes 172056
  66.9 0.0 copy-start.2
  66.9 7.1 %shard_map.79 = f32[1,896,4096]{2,1,0:T(8,128)} custom-call(bf16[96,896]{1,0:T(8,128)(2,1)S(1)} %copy-done.3, bf16[1,96,4096]{2,1,0:T(8,128)(2,1)S(1)} %bitcast.6), custom_call_target="tpu_custom_call" | custom-call | tf_op jit(solution)/shard_map/pallas_call | solution.py:373
  74.0 0.0 copy-done
  74.0 0.0 copy-done.2
  74.0 13.9 %shard_map.78 = f32[2,4096,896]{2,1,0:T(8,128)} custom-call(bf16[96,4096]{1,0:T(8,128)(2,1)S(1)} %copy-done, bf16[2,96,896]{2,1,0:T(8,128)(2,1)S(1)} %copy-done.2), custom_call_target="tpu_custom_call" | custom-call | tf_op jit(solution)/shard_map/pallas_call | solution.py:373
Async XLA Ops:
  64.7 9.3 %copy-start = (bf16[96,4096]{1,0:T(8,128)(2,1)S(1)}, bf16[96,4096]{1,0:T(8,128)(2,1)}, u32[]{:S(2)}) copy-start(bf16[96,4096]{1,0:T(8,128)(2,1)} %a_ref.1) | copy-start | bytes 2359300
  64.8 1.2 %copy-start.1 = (bf16[96,4096]{1,0:T(8,128)(2,1)S(1)}, bf16[96,4096]{1,0:T(8,128)(2,1)}, u32[]{:S(2)}) copy-start(bf16[96,4096]{1,0:T(8,128)(2,1)} %get-tuple-element.7) | copy-start | bytes 2359300
  66.0 0.9 %copy-start.3 = (bf16[96,896]{1,0:T(8,128)(2,1)S(1)}, bf16[96,896]{1,0:T(8,128)(2,1)}, u32[]{:S(2)}) copy-start(bf16[96,896]{1,0:T(8,128)(2,1)} %get-tuple-element.6.a_ref) | copy-start | bytes 516100
  66.9 7.2 %copy-start.2 = (bf16[2,96,896]{2,1,0:T(8,128)(2,1)S(1)}, bf16[2,96,896]{2,1,0:T(8,128)(2,1)}, u32[]{:S(2)}) copy-start(bf16[2,96,896]{2,1,0:T(8,128)(2,1)} %get-tuple-element.5.b_ref) | copy-start | bytes 1032196

commit v2 on v1

--- a/solution.py
+++ b/solution.py
@@ -73,7 +73,9 @@
     return (grad_gate_up[None], grad_down[None])
 
 
-VMEM_BYTES = 60 * 1024 * 1024
+VMEM_BYTES = 57 * 1024 * 1024
+OUTER_BYTES = 52 * 1024 * 1024
+DOWN_ROWS, UP_ROWS = 128, 512
 AXES = ("group", "dp", "mp")
 NT = (((1,), (1,)), ((), ()))
 TN = (((0,), (0,)), ((), ()))
@@ -87,7 +89,7 @@
     acc_v, acc_p, got_v, got_p, pre_v, ph,
     s_part, s_own, s_got, t_part, t_own, t_got, q_part, q_own, q_got, t_all, o_all, h_acc, h_got,
     wp_sem, pd_sem, wv_sem, vd_sem,
-    av_s, av_r, ap_s, ap_r, s_s, s_r, t_s, t_r, q_s, q_r, b_s, b_r, o_s, o_r, h_s, h_r,
+    av_s, av_r, ap_s, ap_r, s_s, s_r, t_s, t_r, q_s, q_r, b_s, b_r, o_s, o_r, h_s, h_r, f_s,
 ):
     f32, bf16 = jnp.float32, jnp.bfloat16
     index = {axis: lax.axis_index(axis) for axis in AXES}
@@ -274,14 +276,44 @@
             student = student + s_got[other, q].astype(f32)
         o_all[m, q] = ((student - t_all[q].astype(f32)) * loss_scale).astype(bf16)
 
-    o_copies = [
-        send(o_all.at[m], o_all.at[m], o_s.at[step - 1], o_r.at[step - 1], "mp", step)
-        for step in range(1, n_mp)
-    ]
-    for step in range(n_mp):
+    def gather_copy(owner, target, sem):
+        slot = lax.rem(target - owner + n_mp, n_mp) - 1
+        return pltpu.make_async_remote_copy(
+            src_ref=o_all.at[owner], dst_ref=o_all.at[owner],
+            send_sem=sem, recv_sem=o_r.at[slot],
+            device_id={"mp": target}, device_id_type=pl.DeviceIdType.MESH,
+        )
+
+    near = [step for step in (2, 1, *range(3, n_mp)) if step < n_mp]
+    for step in near:
+        z = peer("mp", step)
+
+        @pl.when(jnp.abs(z - m) <= 2)
+        def _():
+            gather_copy(m, z, o_s.at[step - 1]).start()
+
+    def forward(step, act):
+        z = peer("mp", n_mp - step)
+        above = jnp.logical_and(m - z >= 2, m + 1 < n_mp)
+        below = jnp.logical_and(z - m >= 2, m >= 1)
+
+        @pl.when(above)
+        def _():
+            act(gather_copy(z, m + 1, f_s.at[step - 1]))
+
+        @pl.when(below)
+        def _():
+            act(gather_copy(z, m - 1, f_s.at[step - 1]))
+
+    for step in [0] + near:
         z = peer("mp", n_mp - step)
         if step:
-            o_copies[step - 1].wait_recv()
+            pltpu.make_async_remote_copy(
+                src_ref=o_all.at[z], dst_ref=o_all.at[z],
+                send_sem=o_s.at[step - 1], recv_sem=o_r.at[step - 1],
+                device_id={"mp": z}, device_id_type=pl.DeviceIdType.MESH,
+            ).wait_recv()
+            forward(step, lambda copy: copy.start())
 
         @pl.loop(0, n_group)
         def _(q):
@@ -319,6 +351,13 @@
     rows_loop(gradient_rows)
     for copy in sent:
         copy.wait_send()
+    for step in near:
+        z = peer("mp", step)
+
+        @pl.when(jnp.abs(z - m) <= 2)
+        def _():
+            gather_copy(m, z, o_s.at[step - 1]).wait_send()
+        forward(step, lambda copy: copy.wait_send())
 
 
 def layout(sizes, tokens, width, p_units, v_units):
@@ -347,6 +386,7 @@
     counts = [2 * k_steps, down, 2 * k_steps, down]
     for n in (d2, d2, m1, g1, m1, g1, m1, d1):
         counts += [n, n]
+    counts.append(m1)
     return buffers, [dma((n,)) for n in counts]
 
 
@@ -359,28 +399,71 @@
     buffers, _ = layout(sizes, tokens, width, p_units, v_units)
     held = sum(math.prod(b.shape) * jnp.dtype(b.dtype).itemsize for b in buffers)
     held += 2 * tokens * (2 * width + 3 * v_units)
-    return held <= VMEM_BYTES - 3 * 1024 * 1024
-
-
-def matmul_tn_kernel(a_ref, b_ref, out_ref):
-    out_ref[...] = lax.dot_general(a_ref[...], b_ref[...], TN, preferred_element_type=jnp.float32)
-
-
-def outer_product(a, b, rows):
-    tokens, n_rows = a.shape
-    members, _, n_columns = b.shape
-    rows = math.gcd(n_rows, rows)
+    outer = 12 * width * v_units + 2 * tokens * (2 * width + 3 * v_units)
+    room = 2 * 1024 * 1024
+    return held <= VMEM_BYTES - room and outer <= OUTER_BYTES - room
+
+
+def outer_kernel(
+    hidden_ref, grad_ref, x_ref, pre_grad_ref, down_hbm, up_hbm, down_buf, up_buf, down_sem, up_sem
+):
+    down_tiles, down_rows, _ = down_buf.shape
+    up_tiles, up_rows, _ = up_buf.shape
+    per_member = up_tiles // 2
+
+    def down_copy(i):
+        rows = pl.ds(pl.multiple_of(i * down_rows, down_rows), down_rows)
+        return pltpu.make_async_copy(down_buf.at[i], down_hbm.at[rows], down_sem.at[i])
+
+    def up_copy(i):
+        start = lax.rem(i, per_member) * up_rows
+        rows = pl.ds(pl.multiple_of(start, up_rows), up_rows)
+        return pltpu.make_async_copy(up_buf.at[i], up_hbm.at[i // per_member, rows], up_sem.at[i])
+
+    @pl.loop(0, down_tiles)
+    def _(i):
+        rows = pl.ds(pl.multiple_of(i * down_rows, down_rows), down_rows)
+        down_buf[i] = lax.dot_general(
+            hidden_ref[:, rows], grad_ref[...], TN, preferred_element_type=jnp.float32)
+        down_copy(i).start()
+
+    @pl.loop(0, up_tiles)
+    def _(i):
+        start = lax.rem(i, per_member) * up_rows
+        rows = pl.ds(pl.multiple_of(start, up_rows), up_rows)
+        up_buf[i] = lax.dot_general(
+            x_ref[:, rows], pre_grad_ref[i // per_member], TN, preferred_element_type=jnp.float32)
+        up_copy(i).start()
+
+    @pl.loop(0, down_tiles)
+    def _(i):
+        down_copy(i).wait()
+
+    @pl.loop(0, up_tiles)
+    def _(i):
+        up_copy(i).wait()
+
+
+def outer_products(hidden, output_grad, block_input, pre_grad):
+    units, width = hidden.shape[1], block_input.shape[1]
+    down_rows, up_rows = math.gcd(units, DOWN_ROWS), math.gcd(width, UP_ROWS)
+    vmem, anywhere = pl.BlockSpec(memory_space=pltpu.VMEM), pl.BlockSpec(memory_space=pl.ANY)
     return pl.pallas_call(
-        matmul_tn_kernel,
-        grid=(members, n_rows // rows),
-        out_shape=jax.ShapeDtypeStruct((members, n_rows, n_columns), jnp.float32),
-        in_specs=[
-            pl.BlockSpec((tokens, rows), lambda k, i: (0, i)),
-            pl.BlockSpec((None, tokens, n_columns), lambda k, i: (k, 0, 0)),
+        outer_kernel,
+        out_shape=(
+            jax.ShapeDtypeStruct((units, width), jnp.float32),
+            jax.ShapeDtypeStruct((2, width, units), jnp.float32),
+        ),
+        in_specs=[vmem] * 4,
+        out_specs=(anywhere, anywhere),
+        scratch_shapes=[
+            pltpu.VMEM((units // down_rows, down_rows, width), jnp.float32),
+            pltpu.VMEM((2 * width // up_rows, up_rows, units), jnp.float32),
+            pltpu.SemaphoreType.DMA((units // down_rows,)),
+            pltpu.SemaphoreType.DMA((2 * width // up_rows,)),
         ],
-        out_specs=pl.BlockSpec((None, rows, n_columns), lambda k, i: (k, i, 0)),
-        compiler_params=pltpu.CompilerParams(vmem_limit_bytes=32 * 1024 * 1024),
-    )(a, b)
+        compiler_params=pltpu.CompilerParams(vmem_limit_bytes=OUTER_BYTES),
+    )(hidden, output_grad, block_input, pre_grad)
 
 
 def fused_body(sizes, block_input, parent_gate_up, parent_down, variant_gate_up, variant_down, widths):
@@ -404,9 +487,8 @@
             collective_id=0, has_side_effects=True, vmem_limit_bytes=VMEM_BYTES
         ),
     )(block_input, unit_mask, parent_gate_up, parent_down, variant_gate_up[0], variant_down[0])
-    grad_down = outer_product(hidden, output_grad[None], 128)
-    grad_gate_up = outer_product(block_input, pre_grad, 512)
-    return (grad_gate_up[None], grad_down)
+    grad_down, grad_gate_up = outer_products(hidden, output_grad, block_input, pre_grad)
+    return (grad_gate_up[None], grad_down[None])
 
 
 def body(sizes, *args):

time: 89.4 us -> 82.3 us (0.921); the launches traced: 87.9 us -> 81.8 us
  Pallas kernels: 83.9 us -> 76.9 us
    pallas_call x2 -> x1, Pallas kernels: 21 us -> 15.8 us  [outer_products(): pl.pallas_call(outer_kernel, out_shape=(jax.ShapeDtypeStruct((units, widt...]
    pallas_call x1, Pallas kernels: 62.9 us -> 61 us  [fused_body(): pl.pallas_call(functools.partial(fused_kernel, sizes), out_shape=(jax.Sha...]
    unnamed x8 -> x6, local copies, waits for them, and re-layouts: 2.13 us -> 3.02 us
where the time goes in v2:
time: 82.3 us; the launch traced here: 81.8 us
  Pallas kernels  76.9 us (93%)
  local copies, waits for them, and re-layouts  3.02 us (4%)
  between operations  1.3 us (2%)
    pallas_call x1, Pallas kernels, fused_body(): pl.pallas_call(functools.partial(fused_kernel, sizes), out_shape=(jax.Sha...  61 us
    pallas_call x1, Pallas kernels, outer_products(): pl.pallas_call(outer_kernel, out_shape=(jax.ShapeDtypeStruct((units, widt...  15.8 us
    unnamed x6, local copies, waits for them, and re-layouts  3.02 us

profile of v2, /device:TPU:0, one launch (start us, length us, event | category | flops | bytes accessed | tf_op | source)
XLA Modules:
  0.0 81.8 jit_solution(13609604513422191212)
XLA Ops:
  1.3 0.6 compare_convert_fusion.mask_ref
  1.9 61.0 %shard_map.77 = (bf16[96,896]{1,0:T(8,128)(2,1)}, bf16[96,4096]{1,0:T(8,128)(2,1)}, bf16[2,96,896]{2,1,0:T(8,128)(2,1)}) custom-call(bf16[96,4096]{1,0:T(8,128)(2,1)} %x_ref.3, f32[1,896]{1,0:T(1,128)} %compare_convert_fusion.mask_ref, bf16[2,4096,896]{2,1,0:T(8,128)(2,1)} %wp_hbm.1, bf16[896,4096]{1,0:T(8,128)(2,1)} %pd_hbm.1, ...), custom_call_target="tpu_custom_call" | custom-call | tf_op jit(solution)/shard_map/pallas_call | solution.py:476
  62.9 0.0 copy-start
  62.9 1.1 %copy-done = bf16[96,4096]{1,0:T(8,128)(2,1)S(1)} copy-done((bf16[96,4096]{1,0:T(8,128)(2,1)S(1)}, bf16[96,4096]{1,0:T(8,128)(2,1)}, u32[]{:S(2)}) %copy-start) | copy-done | bytes 786456
  64.0 0.0 copy-start.1
  64.1 1.0 %copy-done.1 = bf16[2,96,896]{2,1,0:T(8,128)(2,1)S(1)} copy-done((bf16[2,96,896]{2,1,0:T(8,128)(2,1)S(1)}, bf16[2,96,896]{2,1,0:T(8,128)(2,1)}, u32[]{:S(2)}) %copy-start.1) | copy-done | bytes 344088
  65.0 0.0 copy-start.2
  65.0 0.9 %copy-done.2 = bf16[96,896]{1,0:T(8,128)(2,1)S(1)} copy-done((bf16[96,896]{1,0:T(8,128)(2,1)S(1)}, bf16[96,896]{1,0:T(8,128)(2,1)}, u32[]{:S(2)}) %copy-start.2) | copy-done | bytes 172056
  65.9 15.8 %shard_map.78 = (f32[896,4096]{1,0:T(8,128)}, f32[2,4096,896]{2,1,0:T(8,128)}) custom-call(bf16[96,896]{1,0:T(8,128)(2,1)S(1)} %copy-done.2, bf16[96,4096]{1,0:T(8,128)(2,1)S(1)} %copy-done, bf16[96,4096]{1,0:T(8,128)(2,1)} %x_ref.3, bf16[2,96,896]{2,1,0:T(8,128)(2,1)S(1)} %copy-done.1), custom_call_target="tpu_custom_call" | custom-call | tf_op jit(solution)/shard_map/pallas_call | solution.py:451
Async XLA Ops:
  62.9 1.1 %copy-start = (bf16[96,4096]{1,0:T(8,128)(2,1)S(1)}, bf16[96,4096]{1,0:T(8,128)(2,1)}, u32[]{:S(2)}) copy-start(bf16[96,4096]{1,0:T(8,128)(2,1)} %get-tuple-element.8.grad_ref) | copy-start | bytes 2359300
  64.0 1.0 %copy-start.1 = (bf16[2,96,896]{2,1,0:T(8,128)(2,1)S(1)}, bf16[2,96,896]{2,1,0:T(8,128)(2,1)}, u32[]{:S(2)}) copy-start(bf16[2,96,896]{2,1,0:T(8,128)(2,1)} %get-tuple-element.9.pre_grad_ref) | copy-start | bytes 1032196
  65.0 0.9 %copy-start.2 = (bf16[96,896]{1,0:T(8,128)(2,1)S(1)}, bf16[96,896]{1,0:T(8,128)(2,1)}, u32[]{:S(2)}) copy-start(bf16[96,896]{1,0:T(8,128)(2,1)} %get-tuple-element.7.hidden_ref) | copy-start | bytes 516100

commit v3 on v2

--- a/solution.py
+++ b/solution.py
@@ -133,9 +133,9 @@
         return pltpu.make_async_copy(hbm.at[rows], buf.at[rows], sem.at[i])
 
     for i in range(2 * k_steps):
-        gate_up_copy(wv_hbm, wv, wv_sem, i).start()
-    for i in range(vd_sem.shape[0]):
-        down_copy(vd_hbm, vd, vd_sem, i).start()
+        gate_up_copy(wp_hbm, wp, wp_sem, i).start()
+    for i in range(pd_sem.shape[0]):
+        down_copy(pd_hbm, pd, pd_sem, i).start()
 
     barrier = pltpu.get_barrier_semaphore()
     for axis in AXES:
@@ -176,43 +176,13 @@
             value = value + got[step * 2 + k, rows, :]
         return value.astype(bf16)
 
-    def start_parent(i):
-        gate_up_copy(wp_hbm, wp, wp_sem, i).start()
-
-    for copy in pre_activations(wv_hbm, wv, wv_sem, acc_v, got_v, av_s, av_r, start_parent):
+    def start_variant(i):
+        gate_up_copy(wv_hbm, wv, wv_sem, i).start()
+
+    for copy in pre_activations(wp_hbm, wp, wp_sem, acc_p, got_p, ap_s, ap_r, start_variant):
         copy.wait_recv()
-    for i in range(pd_sem.shape[0]):
-        down_copy(pd_hbm, pd, pd_sem, i).start()
-
-    def variant_rows(rows):
-        gate, up = total_pre(acc_v, got_v, 0, rows), total_pre(acc_v, got_v, 1, rows)
-        pre_v[0, rows, :] = gate
-        pre_v[1, rows, :] = up
-        gate, up = gate.astype(f32), up.astype(f32)
-        vh_ref[rows, :] = (gate * jax.nn.sigmoid(gate) * up * mask_ref[...]).astype(bf16)
-
-    rows_loop(variant_rows)
     for i in range(vd_sem.shape[0]):
-        down_copy(vd_hbm, vd, vd_sem, i).wait()
-
-    s_copies = []
-    for step in list(range(1, n_mp)) + [0]:
-        z = peer("mp", step)
-
-        @pl.loop(0, n_group)
-        def _(q):
-            term = jnp.dot(vh_ref[...], vd[:, columns(q, z)], preferred_element_type=f32)
-            if step == 0:
-                s_own[q] = term
-            else:
-                s_part[step - 1, q] = term.astype(bf16)
-        if step:
-            s_copies.append(send(
-                s_part.at[step - 1], s_got.at[step - 1], s_s.at[step - 1], s_r.at[step - 1],
-                "mp", step))
-
-    for copy in pre_activations(wp_hbm, wp, wp_sem, acc_p, got_p, ap_s, ap_r, lambda i: None):
-        copy.wait_recv()
+        down_copy(vd_hbm, vd, vd_sem, i).start()
 
     def parent_rows(rows):
         gate = total_pre(acc_p, got_p, 0, rows).astype(f32)
@@ -238,6 +208,8 @@
             t_copies.append(send(
                 t_part.at[step - 1], t_got.at[step - 1], t_s.at[step - 1], t_r.at[step - 1],
                 "group", step))
+
+    a_copies = pre_activations(wv_hbm, wv, wv_sem, acc_v, got_v, av_s, av_r, lambda i: None)
 
     for copy in t_copies:
         copy.wait_recv()
@@ -254,6 +226,36 @@
             q_copies.append(send(
                 q_part.at[step - 1], q_got.at[step - 1], q_s.at[step - 1], q_r.at[step - 1],
                 "mp", step))
+    for copy in a_copies:
+        copy.wait_recv()
+
+    def variant_rows(rows):
+        gate, up = total_pre(acc_v, got_v, 0, rows), total_pre(acc_v, got_v, 1, rows)
+        pre_v[0, rows, :] = gate
+        pre_v[1, rows, :] = up
+        gate, up = gate.astype(f32), up.astype(f32)
+        vh_ref[rows, :] = (gate * jax.nn.sigmoid(gate) * up * mask_ref[...]).astype(bf16)
+
+    rows_loop(variant_rows)
+    for i in range(vd_sem.shape[0]):
+        down_copy(vd_hbm, vd, vd_sem, i).wait()
+
+    s_copies = []
+    for step in list(range(1, n_mp)) + [0]:
+        z = peer("mp", step)
+
+        @pl.loop(0, n_group)
+        def _(q):
+            term = jnp.dot(vh_ref[...], vd[:, columns(q, z)], preferred_element_type=f32)
+            if step == 0:
+                s_own[q] = term
+            else:
+                s_part[step - 1, q] = term.astype(bf16)
+        if step:
+            s_copies.append(send(
+                s_part.at[step - 1], s_got.at[step - 1], s_s.at[step - 1], s_r.at[step - 1],
+                "mp", step))
+
     for copy in q_copies:
         copy.wait_recv()
     value = q_own[...]

time: 82.3 us -> 91.4 us (1.11)
  Pallas kernels: 76.9 us -> 86 us
    pallas_call x1, Pallas kernels: 61 us -> 70.2 us  [fused_body(): pl.pallas_call(functools.partial(fused_kernel, sizes), out_shape=(jax.Sha...]
where the time goes in v3:
time: 91.4 us; the launch traced here: 90.9 us
  Pallas kernels  86 us (94%)
  local copies, waits for them, and re-layouts  3.02 us (3%)
  between operations  1.3 us (1%)
    pallas_call x1, Pallas kernels, fused_body(): pl.pallas_call(functools.partial(fused_kernel, sizes), out_shape=(jax.Sha...  70.2 us
    pallas_call x1, Pallas kernels, outer_products(): pl.pallas_call(outer_kernel, out_shape=(jax.ShapeDtypeStruct((units, widt...  15.8 us
    unnamed x6, local copies, waits for them, and re-layouts  3.02 us

profile of v3, /device:TPU:0, one launch (start us, length us, event | category | flops | bytes accessed | tf_op | source)
XLA Modules:
  0.0 90.9 jit_solution(11368103582279602760)
XLA Ops:
  1.3 0.6 compare_convert_fusion.mask_ref
  1.9 70.2 %shard_map.77 = (bf16[96,896]{1,0:T(8,128)(2,1)}, bf16[96,4096]{1,0:T(8,128)(2,1)}, bf16[2,96,896]{2,1,0:T(8,128)(2,1)}) custom-call(bf16[96,4096]{1,0:T(8,128)(2,1)} %x_ref.3, f32[1,896]{1,0:T(1,128)} %compare_convert_fusion.mask_ref, bf16[2,4096,896]{2,1,0:T(8,128)(2,1)} %wp_hbm.1, bf16[896,4096]{1,0:T(8,128)(2,1)} %pd_hbm.1, ...), custom_call_target="tpu_custom_call" | custom-call | tf_op jit(solution)/shard_map/pallas_call | solution.py:478
  72.1 0.0 copy-start
  72.1 1.1 %copy-done = bf16[96,4096]{1,0:T(8,128)(2,1)S(1)} copy-done((bf16[96,4096]{1,0:T(8,128)(2,1)S(1)}, bf16[96,4096]{1,0:T(8,128)(2,1)}, u32[]{:S(2)}) %copy-start) | copy-done | bytes 786456
  73.2 0.0 copy-start.1
  73.2 1.0 %copy-done.1 = bf16[2,96,896]{2,1,0:T(8,128)(2,1)S(1)} copy-done((bf16[2,96,896]{2,1,0:T(8,128)(2,1)S(1)}, bf16[2,96,896]{2,1,0:T(8,128)(2,1)}, u32[]{:S(2)}) %copy-start.1) | copy-done | bytes 344088
  74.2 0.0 copy-start.2
  74.2 0.9 %copy-done.2 = bf16[96,896]{1,0:T(8,128)(2,1)S(1)} copy-done((bf16[96,896]{1,0:T(8,128)(2,1)S(1)}, bf16[96,896]{1,0:T(8,128)(2,1)}, u32[]{:S(2)}) %copy-start.2) | copy-done | bytes 172056
  75.1 15.8 %shard_map.78 = (f32[896,4096]{1,0:T(8,128)}, f32[2,4096,896]{2,1,0:T(8,128)}) custom-call(bf16[96,896]{1,0:T(8,128)(2,1)S(1)} %copy-done.2, bf16[96,4096]{1,0:T(8,128)(2,1)S(1)} %copy-done, bf16[96,4096]{1,0:T(8,128)(2,1)} %x_ref.3, bf16[2,96,896]{2,1,0:T(8,128)(2,1)S(1)} %copy-done.1), custom_call_target="tpu_custom_call" | custom-call | tf_op jit(solution)/shard_map/pallas_call | solution.py:453
Async XLA Ops:
  72.1 1.1 %copy-start = (bf16[96,4096]{1,0:T(8,128)(2,1)S(1)}, bf16[96,4096]{1,0:T(8,128)(2,1)}, u32[]{:S(2)}) copy-start(bf16[96,4096]{1,0:T(8,128)(2,1)} %get-tuple-element.8.grad_ref) | copy-start | bytes 2359300
  73.2 1.0 %copy-start.1 = (bf16[2,96,896]{2,1,0:T(8,128)(2,1)S(1)}, bf16[2,96,896]{2,1,0:T(8,128)(2,1)}, u32[]{:S(2)}) copy-start(bf16[2,96,896]{2,1,0:T(8,128)(2,1)} %get-tuple-element.9.pre_grad_ref) | copy-start | bytes 1032196
  74.2 0.9 %copy-start.2 = (bf16[96,896]{1,0:T(8,128)(2,1)S(1)}, bf16[96,896]{1,0:T(8,128)(2,1)}, u32[]{:S(2)}) copy-start(bf16[96,896]{1,0:T(8,128)(2,1)} %get-tuple-element.7.hidden_ref) | copy-start | bytes 516100
